TPU v7x, 32 devices: a whole 2x2x4 slice. The times are simulated.
32 devices in a mesh: dp: 4 (over x, core), seq: 8 (over z, y).
Axes of the slice: x: 2, y: 2, z: 4, core: 2. Of those that a mesh axis runs over, the one named last changes fastest.
Arguments:
- queries: bfloat16 [4, 2048, 2048], P('dp', 'seq'), may hold values from -8 to 8
- key_states: bfloat16 [4, 2048, 512], P('dp', 'seq'), may hold values from -6 to 6
- value_states: bfloat16 [4, 2048, 512], P('dp', 'seq'), may hold values from -6 to 6
- block_picks: int32 [4, 3, 8], P('dp'), may hold values from 0 to 1
- out_weight: bfloat16 [2048, 2048], P(('dp', 'seq')), may hold values from -0.5 to 0.5
- out_grad: bfloat16 [4, 2048, 2048], P('dp', 'seq'), may hold values from -4 to 4
Outputs:
- layer_out: bfloat16 [4, 2048, 2048], P('dp', 'seq')
- query_grad: bfloat16 [4, 2048, 2048], P('dp', 'seq')
- key_grad: bfloat16 [4, 2048, 512], P('dp', 'seq')
- value_grad: bfloat16 [4, 2048, 512], P('dp', 'seq')
All inputs are finite; a program needn't handle non-finite values.
Results may differ from a plain program's by a relative error of at most 0.025.
Values may be sent and summed in bfloat16 or wider, within the bound.
A program may use at most 128 MiB of HBM per device.

v0:
```python
import math
import jax
import jax.numpy as jnp
from jax import lax
from jax.sharding import PartitionSpec as P

HEAD_DIM = 128
BLOCK = 128
neg_fill = -1e30


def shifted(block, axis, distance):
    devices = range(lax.axis_size(axis))
    route = [(i - distance, i) for i in devices if i - distance in devices]
    return lax.ppermute(block, axis, route)


def shards(queries, key_states, value_states, block_picks, out_weight, out_grad):
    query_rows = queries[0]
    key_rows = key_states[0]
    value_rows = value_states[0]
    grad_rows = out_grad[0]
    picks_here = block_picks[0]
    tok_count = query_rows.shape[0]
    q_cols = query_rows.shape[1]
    kv_cols = key_rows.shape[1]
    kv_count = kv_cols // HEAD_DIM
    group_size = q_cols // kv_cols
    score_scale = 1.0 / math.sqrt(HEAD_DIM)
    seq_count = lax.axis_size("seq")
    level_count = seq_count.bit_length() - 1
    shard_index = lax.axis_index("seq")
    far_keys = []
    far_values = []
    for level_index in range(level_count):
        distance = 1 << level_index
        got_keys, got_values = shifted((key_rows, value_rows), "seq", distance)
        row_begin = picks_here[level_index, shard_index] * BLOCK
        far_keys.append(lax.dynamic_slice_in_dim(got_keys, row_begin, BLOCK, 0))
        far_values.append(lax.dynamic_slice_in_dim(got_values, row_begin, BLOCK, 0))
    all_keys = jnp.concatenate([key_rows] + far_keys, 0)
    all_values = jnp.concatenate([value_rows] + far_values, 0)
    key_total = all_keys.shape[0]
    row_ids = lax.broadcasted_iota(jnp.int32, (tok_count, key_total), 0)
    col_ids = lax.broadcasted_iota(jnp.int32, (tok_count, key_total), 1)
    far_level = jnp.maximum(col_ids - tok_count, 0) // BLOCK
    far_seen = shard_index >= jnp.left_shift(jnp.int32(1), far_level)
    visible = jnp.where(col_ids < tok_count, col_ids <= row_ids, far_seen)
    whole_weight = lax.all_gather(out_weight, ("dp", "seq"), axis=0, tiled=True)
    attn_grad = lax.dot_general(
        grad_rows, whole_weight, (((1,), (1,)), ((), ())), preferred_element_type=jnp.float32
    )
    attn_grad = attn_grad.astype(jnp.bfloat16)
    query_heads = query_rows.reshape(tok_count, kv_count, group_size, HEAD_DIM)
    key_heads = all_keys.reshape(key_total, kv_count, HEAD_DIM)
    value_heads = all_values.reshape(key_total, kv_count, HEAD_DIM)
    grad_heads = attn_grad.reshape(tok_count, kv_count, group_size, HEAD_DIM)
    attn_parts = []
    dq_parts = []
    dk_parts = []
    dv_parts = []
    for group_index in range(kv_count):
        query_group = query_heads[:, group_index]
        key_group = key_heads[:, group_index]
        value_group = value_heads[:, group_index]
        grad_group = grad_heads[:, group_index]
        scores = (
            jnp.einsum("tgd,sd->gts", query_group, key_group, preferred_element_type=jnp.float32)
            * score_scale
        )
        scores = jnp.where(visible[None], scores, neg_fill)
        row_max = jnp.max(scores, axis=-1, keepdims=True)
        exp_scores = jnp.exp(scores - row_max)
        probs = exp_scores / jnp.sum(exp_scores, axis=-1, keepdims=True)
        probs_low = probs.astype(jnp.bfloat16)
        attn_group = jnp.einsum(
            "gts,sd->tgd", probs_low, value_group, preferred_element_type=jnp.float32
        ).astype(jnp.bfloat16)
        row_delta = jnp.einsum(
            "tgd,tgd->gt", grad_group, attn_group, preferred_element_type=jnp.float32
        )[:, :, None]
        prob_grad = jnp.einsum(
            "tgd,sd->gts", grad_group, value_group, preferred_element_type=jnp.float32
        )
        score_low = (probs * (prob_grad - row_delta)).astype(jnp.bfloat16)
        dq_parts.append(
            (
                jnp.einsum("gts,sd->tgd", score_low, key_group, preferred_element_type=jnp.float32)
                * score_scale
            ).astype(jnp.bfloat16)
        )
        dk_parts.append(
            jnp.einsum("gts,tgd->sd", score_low, query_group, preferred_element_type=jnp.float32)
            * score_scale
        )
        dv_parts.append(
            jnp.einsum("gts,tgd->sd", probs_low, grad_group, preferred_element_type=jnp.float32)
        )
        attn_parts.append(attn_group)
    attn_all = jnp.stack(attn_parts, 1).reshape(tok_count, q_cols)
    query_grad = jnp.stack(dq_parts, 1).reshape(tok_count, q_cols)
    key_terms = jnp.stack(dk_parts, 1).reshape(key_total, kv_cols)
    value_terms = jnp.stack(dv_parts, 1).reshape(key_total, kv_cols)
    layer_sum = jnp.dot(attn_all, whole_weight, preferred_element_type=jnp.float32)
    layer_out = layer_sum.astype(jnp.bfloat16)
    key_grad = key_terms[:tok_count]
    value_grad = value_terms[:tok_count]
    for level_index in range(level_count):
        distance = 1 << level_index
        begin = tok_count + level_index * BLOCK
        back_keys, back_values = shifted(
            (key_terms[begin : begin + BLOCK], value_terms[begin : begin + BLOCK]), "seq", -distance
        )
        source = jnp.minimum(shard_index + distance, seq_count - 1)
        row_begin = picks_here[level_index, source] * BLOCK
        key_grad = lax.dynamic_update_slice_in_dim(
            key_grad,
            lax.dynamic_slice_in_dim(key_grad, row_begin, BLOCK, 0) + back_keys,
            row_begin,
            0,
        )
        value_grad = lax.dynamic_update_slice_in_dim(
            value_grad,
            lax.dynamic_slice_in_dim(value_grad, row_begin, BLOCK, 0) + back_values,
            row_begin,
            0,
        )
    return (
        layer_out[None],
        query_grad[None],
        key_grad.astype(jnp.bfloat16)[None],
        value_grad.astype(jnp.bfloat16)[None],
    )


def solution(mesh):
    return jax.shard_map(
        shards,
        mesh=mesh,
        in_specs=(
            P("dp", "seq", None),
            P("dp", "seq", None),
            P("dp", "seq", None),
            P("dp", None, None),
            P(("dp", "seq"), None),
            P("dp", "seq", None),
        ),
        out_specs=(
            P("dp", "seq", None),
            P("dp", "seq", None),
            P("dp", "seq", None),
            P("dp", "seq", None),
        ),
        check_vma=False,
    )
```

profile of v0, /device:TPU:0, one launch (start us, length us, event | category | flops | bytes accessed | tf_op | source)
XLA Modules:
  0.0 234.0 jit_solution(6987228526842534962)
XLA Ops:
  9.0 6.0 %collective-permute-start.5 = (bf16[256,512]{0,1:T(8,128)(2,1)S(1)}, bf16[256,512]{0,1:T(8,128)(2,1)S(1)}, u32[]{:S(2)}, u32[]{:S(2)}) collective-permute-start(bf16[256,512]{0,1:T(8,128)(2,1)S(1)} %bitcast.364), channel_id=1, source_target_pairs={{0,4},{1,5},{2,6},{3,7},{8,12},{9,13},{10,14},{11,15},{16,20},{17,... | collective-permute-start | bytes 786440 | tf_op jit(solution)/shard_map/ppermute | solution.py:15
  15.0 4.2 %collective-permute-start.4 = (bf16[256,512]{0,1:T(8,128)(2,1)S(1)}, bf16[256,512]{0,1:T(8,128)(2,1)}, u32[]{:S(2)}, u32[]{:S(2)}) collective-permute-start(bf16[256,512]{0,1:T(8,128)(2,1)S(1)} %bitcast.365), channel_id=1, source_target_pairs={{0,2},{1,3},{2,4},{3,5},{4,6},{5,7},{8,10},{9,11},{10,12},{11,13},... | collective-permute-start | bytes 786440 | tf_op jit(solution)/shard_map/ppermute | solution.py:15
  19.2 3.4 %collective-permute-start.3 = (bf16[256,512]{0,1:T(8,128)(2,1)S(1)}, bf16[256,512]{0,1:T(8,128)(2,1)S(1)}, u32[]{:S(2)}, u32[]{:S(2)}) collective-permute-start(bf16[256,512]{0,1:T(8,128)(2,1)S(1)} %bitcast.366), channel_id=1, source_target_pairs={{0,1},{1,2},{2,3},{3,4},{4,5},{5,6},{6,7},{8,9},{9,10},{10,11},{11... | collective-permute-start | bytes 786440 | tf_op jit(solution)/shard_map/ppermute | solution.py:15
  22.6 2.0 collective-permute-start.2
  24.6 2.0 collective-permute-start.1
  26.6 1.3 fusion.50
  28.0 1.4 constant_dynamic-slice_fusion
  34.4 1.5 copy.71
  35.9 2.6 %collective-permute-start = (bf16[256,512]{1,0:T(8,128)(2,1)}, bf16[256,512]{1,0:T(8,128)(2,1)}, u32[]{:S(2)}, u32[]{:S(2)}) collective-permute-start(bf16[256,512]{1,0:T(8,128)(2,1)} %bitcast.9), channel_id=1, source_target_pairs={{0,1},{1,2},{2,3},{3,4},{4,5},{5,6},{6,7},{8,9},{9,10},{10,11},{11... | collective-permute-start | bytes 786440 | tf_op jit(solution)/shard_map/ppermute | solution.py:15
  48.6 2.5 %fusion.92 = (f32[4,256]{1,0:T(4,128)S(1)}, f32[4,256,640]{1,2,0:T(8,128)}) fusion(pred[256,640]{0,1:T(8,128)(4,1)S(1)} %copy-done.44, bf16[256,4,4,128]{0,3,2,1:T(8,128)(2,1)S(1)} %bitcast.353, bf16[640,4,128]{2,0,1:T(8,128)(2,1)S(1)} %pad_maximum_fusion.5), kind=kOutput, calls=%fused_computation.181 | convolution fusion | flops 170394240 | bytes 3215360 | tf_op jit(solution)/shard_map/sub | solution.py:73
  51.1 2.4 %fusion.93 = (f32[4,256]{1,0:T(4,128)S(1)}, f32[4,256,640]{1,2,0:T(8,128)}) fusion(pred[256,640]{0,1:T(8,128)(4,1)S(1)} %copy-done.44, bf16[256,4,4,128]{0,3,2,1:T(8,128)(2,1)S(1)} %bitcast.354, bf16[640,4,128]{2,0,1:T(8,128)(2,1)S(1)} %pad_maximum_fusion.5), kind=kOutput, calls=%fused_computation.182 | convolution fusion | flops 170394240 | bytes 3215360 | tf_op jit(solution)/shard_map/sub | solution.py:73
  53.5 2.5 %fusion.90 = (f32[4,256]{1,0:T(4,128)S(1)}, f32[4,256,640]{1,2,0:T(8,128)}) fusion(pred[256,640]{0,1:T(8,128)(4,1)S(1)} %copy-done.44, bf16[256,4,4,128]{0,3,2,1:T(8,128)(2,1)S(1)} %bitcast.355, bf16[640,4,128]{2,0,1:T(8,128)(2,1)S(1)} %pad_maximum_fusion.5), kind=kOutput, calls=%fused_computation.179 | convolution fusion | flops 170394240 | bytes 3215360 | tf_op jit(solution)/shard_map/sub | solution.py:73
  56.1 2.5 %fusion.91 = (f32[4,256]{1,0:T(4,128)S(1)}, f32[4,256,640]{1,2,0:T(8,128)}) fusion(pred[256,640]{0,1:T(8,128)(4,1)S(1)} %copy-done.44, bf16[256,4,4,128]{0,3,2,1:T(8,128)(2,1)S(1)} %bitcast.356, bf16[640,4,128]{2,0,1:T(8,128)(2,1)S(1)} %pad_maximum_fusion.5), kind=kOutput, calls=%fused_computation.180 | convolution fusion | flops 170394240 | bytes 3215360 | tf_op jit(solution)/shard_map/sub | solution.py:73
  58.5 3.2 %fusion.46 = bf16[4,256,640]{1,2,0:T(8,128)(2,1)} fusion(f32[4,256,640]{1,2,0:T(8,128)} %get-tuple-element.33, f32[4,256]{1,0:T(4,128)S(1)} %get-tuple-element.32), kind=kLoop, calls=%fused_computation.82 | loop fusion | flops 1310720 | bytes 3936256 | tf_op jit(solution)/shard_map/convert_element_type | solution.py:75
  61.7 1.3 fusion.45
  64.0 1.3 fusion.48
  66.4 39.2 %all-gather.2.cloned.1.call-done = bf16[2048,2048]{1,0:T(8,128)(2,1)} async-done(((bf16[64,2048]{1,0:T(8,128)(2,1)}), bf16[2048,2048]{1,0:T(8,128)(2,1)}) %all-gather.2.cloned.1.call-update) | async-done | bytes 8388624 | tf_op jit(solution)/shard_map/all_gather | solution.py:49
  105.6 6.7 %convolution_convert_fusion = bf16[256,2048]{1,0:T(8,128)(2,1)} fusion(bf16[2048,2048]{1,0:T(8,128)(2,1)} %all-gather.2.cloned.1.call-done, bf16[1,256,2048]{2,1,0:T(8,128)(2,1)S(1)} %copy-done), kind=kOutput, calls=%fused_computation.24 | convolution fusion | flops 2148007936 | bytes 10485760 | tf_op jit(solution)/shard_map/dot_general | solution.py:50
  112.3 1.8 reshape.144
  116.5 2.1 copy.142
  118.7 2.8 %convolution_bitcast_fusion.2 = f32[640,1,128]{0,2,1:T(8,128)} fusion(bf16[4,256,640]{1,2,0:T(8,128)(2,1)} %fusion.46, bf16[256,1,4,128]{3,2,1,0:T(4,128)(2,1)} %copy-done.27), kind=kOutput, calls=%fused_computation.63 | convolution fusion | flops 167772160 | bytes 1900544 | tf_op jit(solution)/shard_map/gts,tgd->sd/dot_general | solution.py:97
  121.5 2.1 multiply_reduce_fusion.2
  124.2 2.1 fusion.43
  127.6 2.0 copy.133
  129.6 2.8 %convolution_bitcast_fusion.3 = f32[640,1,128]{0,2,1:T(8,128)} fusion(bf16[4,256,640]{1,2,0:T(8,128)(2,1)} %fusion.45, bf16[256,1,4,128]{3,2,1,0:T(4,128)(2,1)} %copy-done.26), kind=kOutput, calls=%fused_computation.64 | convolution fusion | flops 167772160 | bytes 1900544 | tf_op jit(solution)/shard_map/gts,tgd->sd/dot_general | solution.py:97
  132.4 2.2 multiply_reduce_fusion.3
  134.7 1.6 fusion.11
  136.2 2.0 fusion.44
  140.6 2.0 copy.160
  142.6 2.8 %convolution_bitcast_fusion = f32[640,1,128]{0,2,1:T(8,128)} fusion(bf16[4,256,640]{1,2,0:T(8,128)(2,1)} %fusion.48, bf16[256,1,4,128]{3,2,1,0:T(4,128)(2,1)} %get-tuple-element.21), kind=kOutput, calls=%fused_computation.61 | convolution fusion | flops 167772160 | bytes 1900544 | tf_op jit(solution)/shard_map/gts,tgd->sd/dot_general | solution.py:97
  145.4 2.2 multiply_reduce_fusion
  147.6 1.6 fusion.5
  149.2 2.0 fusion.41
  152.5 2.0 copy.151
  154.6 2.4 %convolution_bitcast_fusion.1 = f32[640,1,128]{0,2,1:T(8,128)} fusion(bf16[4,256,640]{1,2,0:T(8,128)(2,1)S(1)} %fusion.47, bf16[256,1,4,128]{3,2,1,0:T(4,128)(2,1)} %get-tuple-element.19), kind=kOutput, calls=%fused_computation.62 | convolution fusion | flops 167772160 | bytes 1900544 | tf_op jit(solution)/shard_map/gts,tgd->sd/dot_general | solution.py:97
  157.0 2.2 multiply_reduce_fusion.1
  160.2 2.1 fusion.42
  165.3 1.4 collective-permute-start.6
  167.7 1.8 copy.118
  171.0 6.7 %fusion.12 = bf16[1,256,2048]{2,1,0:T(8,128)(2,1)} fusion(bf16[256,2048]{0,1:T(8,128)(2,1)S(1)} %bitcast.351, bf16[2048,2048]{1,0:T(8,128)(2,1)} %all-gather.2.cloned.1.call-done), kind=kOutput, calls=%fused_computation.26 | convolution fusion | flops 2148007936 | bytes 10485760 | tf_op jit(solution)/shard_map/dot_general | solution.py:104
  179.5 1.4 copy.122
  182.9 1.4 collective-permute-start.7
  184.3 1.3 collective-permute-start.8
  187.4 1.3 collective-permute-start.11
  190.7 6.3 %collective-permute-done.7 = f32[128,512]{1,0:T(8,128)} collective-permute-done((f32[128,512]{1,0:T(8,128)}, f32[128,512]{1,0:T(8,128)}, u32[]{:S(2)}, u32[]{:S(2)}) %collective-permute-start.7) | collective-permute-done | bytes 262176 | tf_op jit(solution)/shard_map/ppermute | solution.py:15
  198.1 5.3 %collective-permute-done.10 = f32[128,512]{1,0:T(8,128)S(1)} collective-permute-done((f32[128,512]{1,0:T(8,128)S(1)}, f32[128,512]{1,0:T(8,128)S(1)}, u32[]{:S(2)}, u32[]{:S(2)}) %collective-permute-start.10) | collective-permute-done | bytes 262176 | tf_op jit(solution)/shard_map/ppermute | solution.py:15
  203.5 8.4 %collective-permute-done.8 = f32[128,512]{1,0:T(8,128)} collective-permute-done((f32[128,512]{1,0:T(8,128)S(1)}, f32[128,512]{1,0:T(8,128)}, u32[]{:S(2)}, u32[]{:S(2)}) %collective-permute-start.8) | collective-permute-done | bytes 262176 | tf_op jit(solution)/shard_map/ppermute | solution.py:15
  213.6 12.8 %collective-permute-done.11 = f32[128,512]{1,0:T(8,128)S(1)} collective-permute-done((f32[128,512]{1,0:T(8,128)S(1)}, f32[128,512]{1,0:T(8,128)S(1)}, u32[]{:S(2)}, u32[]{:S(2)}) %collective-permute-start.11) | collective-permute-done | bytes 262176 | tf_op jit(solution)/shard_map/ppermute | solution.py:15
  (156 shorter events, 40.3 us)
Async XLA Ops:
  7.2 98.5 %copy-start = (bf16[1,256,2048]{2,1,0:T(8,128)(2,1)S(1)}, bf16[1,256,2048]{2,1,0:T(8,128)(2,1)}, u32[]{:S(2)}) copy-start(bf16[1,256,2048]{2,1,0:T(8,128)(2,1)} %param.11) | copy-start | bytes 3145732
  7.2 98.4 %all-gather.2.cloned.1.call-start = ((), (), s32[]{:S(2)}) async-start(), calls=%async_computation | async-start | bytes 8650752 | tf_op jit(solution)/shard_map/all_gather | solution.py:49
  9.0 26.9 %collective-permute-start.5 = (bf16[256,512]{0,1:T(8,128)(2,1)S(1)}, bf16[256,512]{0,1:T(8,128)(2,1)S(1)}, u32[]{:S(2)}, u32[]{:S(2)}) collective-permute-start(bf16[256,512]{0,1:T(8,128)(2,1)S(1)} %bitcast.364), channel_id=1, source_target_pairs={{0,4},{1,5},{2,6},{3,7},{8,12},{9,13},{10,14},{11,15},{16,20},{17,... | collective-permute-start | bytes 786440 | tf_op jit(solution)/shard_map/ppermute | solution.py:15
  15.0 23.6 %collective-permute-start.4 = (bf16[256,512]{0,1:T(8,128)(2,1)S(1)}, bf16[256,512]{0,1:T(8,128)(2,1)}, u32[]{:S(2)}, u32[]{:S(2)}) collective-permute-start(bf16[256,512]{0,1:T(8,128)(2,1)S(1)} %bitcast.365), channel_id=1, source_target_pairs={{0,2},{1,3},{2,4},{3,5},{4,6},{5,7},{8,10},{9,11},{10,12},{11,13},... | collective-permute-start | bytes 786440 | tf_op jit(solution)/shard_map/ppermute | solution.py:15
  19.2 20.3 %collective-permute-start.3 = (bf16[256,512]{0,1:T(8,128)(2,1)S(1)}, bf16[256,512]{0,1:T(8,128)(2,1)S(1)}, u32[]{:S(2)}, u32[]{:S(2)}) collective-permute-start(bf16[256,512]{0,1:T(8,128)(2,1)S(1)} %bitcast.366), channel_id=1, source_target_pairs={{0,1},{1,2},{2,3},{3,4},{4,5},{5,6},{6,7},{8,9},{9,10},{10,11},{11... | collective-permute-start | bytes 786440 | tf_op jit(solution)/shard_map/ppermute | solution.py:15
  22.6 18.0 %collective-permute-start.2 = (bf16[256,512]{1,0:T(8,128)(2,1)}, bf16[256,512]{1,0:T(8,128)(2,1)}, u32[]{:S(2)}, u32[]{:S(2)}) collective-permute-start(bf16[256,512]{1,0:T(8,128)(2,1)} %bitcast.9), channel_id=1, source_target_pairs={{0,4},{1,5},{2,6},{3,7},{8,12},{9,13},{10,14},{11,15},{16,20},{17,... | collective-permute-start | bytes 786440 | tf_op jit(solution)/shard_map/ppermute | solution.py:15
  24.6 18.5 %collective-permute-start.1 = (bf16[256,512]{1,0:T(8,128)(2,1)}, bf16[256,512]{1,0:T(8,128)(2,1)}, u32[]{:S(2)}, u32[]{:S(2)}) collective-permute-start(bf16[256,512]{1,0:T(8,128)(2,1)} %bitcast.9), channel_id=1, source_target_pairs={{0,2},{1,3},{2,4},{3,5},{4,6},{5,7},{8,10},{9,11},{10,12},{11,13},... | collective-permute-start | bytes 786440 | tf_op jit(solution)/shard_map/ppermute | solution.py:15
  35.9 20.2 %copy-start.4 = (bf16[1,256,2048]{1,2,0:T(8,128)(2,1)}, bf16[1,256,2048]{1,2,0:T(8,128)(2,1)S(1)}, u32[]{:S(2)}) copy-start(bf16[1,256,2048]{1,2,0:T(8,128)(2,1)S(1)} %copy.71) | copy-start | bytes 3145732
  35.9 8.8 %collective-permute-start = (bf16[256,512]{1,0:T(8,128)(2,1)}, bf16[256,512]{1,0:T(8,128)(2,1)}, u32[]{:S(2)}, u32[]{:S(2)}) collective-permute-start(bf16[256,512]{1,0:T(8,128)(2,1)} %bitcast.9), channel_id=1, source_target_pairs={{0,1},{1,2},{2,3},{3,4},{4,5},{5,6},{6,7},{8,9},{9,10},{10,11},{11... | collective-permute-start | bytes 786440 | tf_op jit(solution)/shard_map/ppermute | solution.py:15
  47.5 8.6 %copy-start.22 = (bf16[640,4,128]{2,0,1:T(8,128)(2,1)}, bf16[640,4,128]{2,0,1:T(8,128)(2,1)S(1)}, u32[]{:S(2)}) copy-start(bf16[640,4,128]{2,0,1:T(8,128)(2,1)S(1)} %pad_maximum_fusion.5) | copy-start | bytes 1966084
  58.5 3.2 %copy-start.19 = (f32[4,256,640]{1,2,0:T(8,128)S(1)}, f32[4,256,640]{1,2,0:T(8,128)}, u32[]{:S(2)}) copy-start(f32[4,256,640]{1,2,0:T(8,128)} %get-tuple-element.35) | copy-start | bytes 7864324
  61.7 2.2 copy-start.17
  64.0 2.2 copy-start.15
  116.5 5.0 %copy-start.13 = (bf16[640,4,128]{0,2,1:T(8,128)(2,1)S(1)}, bf16[640,4,128]{0,2,1:T(8,128)(2,1)}, u32[]{:S(2)}) copy-start(bf16[640,4,128]{0,2,1:T(8,128)(2,1)} %pad_maximum_fusion.4) | copy-start | bytes 1966084
  116.5 7.1 %copy-start.28 = (bf16[256,1,4,128]{3,2,1,0:T(4,128)(2,1)S(1)}, bf16[256,1,4,128]{3,2,1,0:T(4,128)(2,1)}, u32[]{:S(2)}) copy-start(bf16[256,1,4,128]{3,2,1,0:T(4,128)(2,1)} %copy-done.27) | copy-start | bytes 786436
  118.7 2.8 %copy-start.3 = (bf16[4,256,640]{1,2,0:T(8,128)(2,1)S(1)}, bf16[4,256,640]{1,2,0:T(8,128)(2,1)}, u32[]{:S(2)}) copy-start(bf16[4,256,640]{1,2,0:T(8,128)(2,1)} %fusion.46) | copy-start | bytes 3932164
  118.7 4.9 %copy-start.21 = (f32[4,256,640]{1,2,0:T(8,128)S(1)}, f32[4,256,640]{1,2,0:T(8,128)}, u32[]{:S(2)}) copy-start(f32[4,256,640]{1,2,0:T(8,128)} %get-tuple-element.33) | copy-start | bytes 7864324
  124.1 2.1 copy-start.5
  129.6 2.8 %copy-start.2 = (bf16[4,256,640]{1,2,0:T(8,128)(2,1)S(1)}, bf16[4,256,640]{1,2,0:T(8,128)(2,1)}, u32[]{:S(2)}) copy-start(bf16[4,256,640]{1,2,0:T(8,128)(2,1)} %fusion.45) | copy-start | bytes 3932164
  129.6 5.1 %copy-start.20 = (f32[4,256,640]{1,2,0:T(8,128)S(1)}, f32[4,256,640]{1,2,0:T(8,128)}, u32[]{:S(2)}) copy-start(f32[4,256,640]{1,2,0:T(8,128)} %get-tuple-element.35) | copy-start | bytes 7864324
  142.6 2.8 %copy-start.1 = (bf16[4,256,640]{1,2,0:T(8,128)(2,1)S(1)}, bf16[4,256,640]{1,2,0:T(8,128)(2,1)}, u32[]{:S(2)}) copy-start(bf16[4,256,640]{1,2,0:T(8,128)(2,1)} %fusion.48) | copy-start | bytes 3932164
  142.6 5.0 %copy-start.18 = (f32[4,256,640]{1,2,0:T(8,128)S(1)}, f32[4,256,640]{1,2,0:T(8,128)}, u32[]{:S(2)}) copy-start(f32[4,256,640]{1,2,0:T(8,128)} %get-tuple-element.29) | copy-start | bytes 7864324
  154.6 2.4 %copy-start.14 = (bf16[640,4,128]{0,2,1:T(8,128)(2,1)S(1)}, bf16[640,4,128]{0,2,1:T(8,128)(2,1)}, u32[]{:S(2)}) copy-start(bf16[640,4,128]{0,2,1:T(8,128)(2,1)} %pad_maximum_fusion.4) | copy-start | bytes 1966084
  154.6 4.6 %copy-start.16 = (f32[4,256,640]{1,2,0:T(8,128)S(1)}, f32[4,256,640]{1,2,0:T(8,128)}, u32[]{:S(2)}) copy-start(f32[4,256,640]{1,2,0:T(8,128)} %get-tuple-element.31) | copy-start | bytes 7864324
  157.0 2.2 copy-start.24
  160.2 2.1 copy-start.9
  160.2 2.1 copy-start.11
  160.2 2.1 copy-start.12
  163.3 3.5 %copy-start.6 = (f32[640,1,128]{0,2,1:T(8,128)S(1)}, f32[640,1,128]{0,2,1:T(8,128)}, u32[]{:S(2)}) copy-start(f32[640,1,128]{0,2,1:T(8,128)} %convolution_bitcast_fusion.2) | copy-start | bytes 983044
  163.3 3.5 %copy-start.7 = (f32[640,1,128]{0,2,1:T(8,128)S(1)}, f32[640,1,128]{0,2,1:T(8,128)}, u32[]{:S(2)}) copy-start(f32[640,1,128]{0,2,1:T(8,128)} %convolution_bitcast_fusion.3) | copy-start | bytes 983044
  163.3 3.5 %copy-start.8 = (f32[640,1,128]{0,2,1:T(8,128)S(1)}, f32[640,1,128]{0,2,1:T(8,128)}, u32[]{:S(2)}) copy-start(f32[640,1,128]{0,2,1:T(8,128)} %convolution_bitcast_fusion) | copy-start | bytes 983044
  163.3 3.5 %copy-start.10 = (f32[640,1,128]{0,2,1:T(8,128)S(1)}, f32[640,1,128]{0,2,1:T(8,128)}, u32[]{:S(2)}) copy-start(f32[640,1,128]{0,2,1:T(8,128)} %convolution_bitcast_fusion.1) | copy-start | bytes 983044
  165.3 5.5 %copy-start.29 = (bf16[128,4,256]{2,0,1:T(8,128)(2,1)S(1)}, bf16[128,4,256]{2,0,1:T(8,128)(2,1)}, u32[]{:S(2)}) copy-start(bf16[128,4,256]{2,0,1:T(8,128)(2,1)} %get-tuple-element.41) | copy-start | bytes 786436
  165.3 5.5 %copy-start.30 = (bf16[128,4,256]{2,0,1:T(8,128)(2,1)S(1)}, bf16[128,4,256]{2,0,1:T(8,128)(2,1)}, u32[]{:S(2)}) copy-start(bf16[128,4,256]{2,0,1:T(8,128)(2,1)} %get-tuple-element.43) | copy-start | bytes 786436
  165.3 5.5 %copy-start.31 = (bf16[128,4,256]{2,0,1:T(8,128)(2,1)S(1)}, bf16[128,4,256]{2,0,1:T(8,128)(2,1)}, u32[]{:S(2)}) copy-start(bf16[128,4,256]{2,0,1:T(8,128)(2,1)} %get-tuple-element.37) | copy-start | bytes 786436
  165.3 5.5 %copy-start.32 = (bf16[128,4,256]{2,0,1:T(8,128)(2,1)S(1)}, bf16[128,4,256]{2,0,1:T(8,128)(2,1)}, u32[]{:S(2)}) copy-start(bf16[128,4,256]{2,0,1:T(8,128)(2,1)} %get-tuple-element.39) | copy-start | bytes 786436
  165.3 22.1 %collective-permute-start.6 = (f32[128,512]{1,0:T(8,128)}, f32[128,512]{1,0:T(8,128)}, u32[]{:S(2)}, u32[]{:S(2)}) collective-permute-start(f32[128,512]{1,0:T(8,128)} %copy.105), channel_id=1, source_target_pairs={{1,0},{2,1},{3,2},{4,3},{5,4},{6,5},{7,6},{9,8},{10,9},{11,10},{12... | collective-permute-start | bytes 786440 | tf_op jit(solution)/shard_map/ppermute | solution.py:15
  169.5 20.2 %collective-permute-start.9 = (f32[128,512]{1,0:T(8,128)}, f32[128,512]{1,0:T(8,128)}, u32[]{:S(2)}, u32[]{:S(2)}) collective-permute-start(f32[128,512]{1,0:T(8,128)} %copy.118), channel_id=1, source_target_pairs={{1,0},{2,1},{3,2},{4,3},{5,4},{6,5},{7,6},{9,8},{10,9},{11,10},{12... | collective-permute-start | bytes 786440 | tf_op jit(solution)/shard_map/ppermute | solution.py:15
  177.7 1.4 copy-start.39
  177.7 1.7 copy-start.40
  179.5 1.4 slice-start
  181.1 4.5 %slice-start.1 = ((f32[640,4,128]{0,2,1:T(8,128)}), f32[256,4,128]{0,2,1:T(8,128)S(1)}, s32[]{:S(2)}) async-start(f32[640,4,128]{0,2,1:T(8,128)} %pad_maximum_fusion.1), calls=%async_computation.2 | async-start | bytes 1048576 | tf_op jit(solution)/shard_map/slice | solution.py:107
  182.0 3.8 %copy-start.34 = (f32[128,4,128]{0,2,1:T(8,128)S(1)}, f32[128,4,128]{0,2,1:T(8,128)}, u32[]{:S(2)}) copy-start(f32[128,4,128]{0,2,1:T(8,128)} %get-tuple-element.12) | copy-start | bytes 786436
  182.9 3.1 %copy-start.33 = (f32[128,4,128]{0,2,1:T(8,128)S(1)}, f32[128,4,128]{0,2,1:T(8,128)}, u32[]{:S(2)}) copy-start(f32[128,4,128]{0,2,1:T(8,128)} %get-tuple-element.13) | copy-start | bytes 786436
  182.9 14.2 %collective-permute-start.7 = (f32[128,512]{1,0:T(8,128)}, f32[128,512]{1,0:T(8,128)}, u32[]{:S(2)}, u32[]{:S(2)}) collective-permute-start(f32[128,512]{1,0:T(8,128)} %copy.107), channel_id=1, source_target_pairs={{2,0},{3,1},{4,2},{5,3},{6,4},{7,5},{10,8},{11,9},{12,10},{13,11},... | collective-permute-start | bytes 786440 | tf_op jit(solution)/shard_map/ppermute | solution.py:15
  184.3 27.6 %collective-permute-start.8 = (f32[128,512]{1,0:T(8,128)S(1)}, f32[128,512]{1,0:T(8,128)}, u32[]{:S(2)}, u32[]{:S(2)}) collective-permute-start(f32[128,512]{1,0:T(8,128)S(1)} %copy.108), channel_id=1, source_target_pairs={{4,0},{5,1},{6,2},{7,3},{12,8},{13,9},{14,10},{15,11},{20,16},{21,... | collective-permute-start | bytes 786440 | tf_op jit(solution)/shard_map/ppermute | solution.py:15
  186.1 17.3 %collective-permute-start.10 = (f32[128,512]{1,0:T(8,128)S(1)}, f32[128,512]{1,0:T(8,128)S(1)}, u32[]{:S(2)}, u32[]{:S(2)}) collective-permute-start(f32[128,512]{1,0:T(8,128)S(1)} %copy.120), channel_id=1, source_target_pairs={{2,0},{3,1},{4,2},{5,3},{6,4},{7,5},{10,8},{11,9},{12,10},{13,11},... | collective-permute-start | bytes 786440 | tf_op jit(solution)/shard_map/ppermute | solution.py:15
  187.4 39.0 %collective-permute-start.11 = (f32[128,512]{1,0:T(8,128)S(1)}, f32[128,512]{1,0:T(8,128)S(1)}, u32[]{:S(2)}, u32[]{:S(2)}) collective-permute-start(f32[128,512]{1,0:T(8,128)S(1)} %copy.121), channel_id=1, source_target_pairs={{4,0},{5,1},{6,2},{7,3},{12,8},{13,9},{14,10},{15,11},{20,16},{21,... | collective-permute-start | bytes 786440 | tf_op jit(solution)/shard_map/ppermute | solution.py:15
  (12 other events, 13.7 us)
Sparse Core Ops, SparseCore 0:
  11.0 94.5 all-gather.1
where the time goes:
time: 235 us; the launch traced here: 234 us
  waiting for transfers between devices  73.5 us (31%)
  matrix products  59.8 us (25%)
  local copies, waits for them, and re-layouts  32.5 us (14%)
  starting transfers between devices  28.3 us (12%)
  other arithmetic  21.5 us (9%)
  between operations  18.4 us (8%)
    all_gather x1, waiting for transfers between devices, shards(): whole_weight = lax.all_gather(out_weight, ('dp', 'seq'), axis=0, tiled=True)  39.2 us
    ppermute x12, waiting for transfers between devices, shifted(): return lax.ppermute(block, axis, route)  33.7 us
    ppermute x12, starting transfers between devices, shifted(): return lax.ppermute(block, axis, route)  28.2 us
    unnamed x98, local copies, waits for them, and re-layouts  16.7 us
    dot_general x4, matrix products, shards(): jnp.einsum('gts,tgd->sd', probs_low, grad_group, preferred_element_type=j...  10.9 us
    sub x4, matrix products, shards(): exp_scores = jnp.exp(scores - row_max)  9.91 us
    dot_general x4, matrix products, shards(): jnp.einsum('gts,sd->tgd', probs_low, value_group, preferred_element_type=...  8.71 us
    dot_general x4, matrix products, shards(): jnp.einsum('gts,sd->tgd', score_low, key_group, preferred_element_type=jn...  8.28 us
  transfers between devices with their start and end apart: 13, of which 6 were waited for; matrix products, arithmetic and copies ran while one was open for 21% of the time, Pallas kernels for 0%

commit v1 on v0

--- a/solution.py
+++ b/solution.py
@@ -7,6 +7,18 @@
 HEAD_DIM = 128
 BLOCK = 128
 neg_fill = -1e30
+
+
+def gather_by_bits(x, axis, dim):
+    ways, here = (lax.axis_size(axis), lax.axis_index(axis))
+    grown, reach = (x, 1)
+    while reach < ways:
+        theirs = lax.ppermute(grown, axis, [(d, d ^ reach) for d in range(ways)])
+        mine_first = jnp.concatenate([grown, theirs], axis=dim)
+        theirs_first = jnp.concatenate([theirs, grown], axis=dim)
+        grown = jnp.where(here & reach == 0, mine_first, theirs_first)
+        reach = 2 * reach
+    return grown
 
 
 def shifted(block, axis, distance):
@@ -46,7 +58,7 @@
     far_level = jnp.maximum(col_ids - tok_count, 0) // BLOCK
     far_seen = shard_index >= jnp.left_shift(jnp.int32(1), far_level)
     visible = jnp.where(col_ids < tok_count, col_ids <= row_ids, far_seen)
-    whole_weight = lax.all_gather(out_weight, ("dp", "seq"), axis=0, tiled=True)
+    whole_weight = gather_by_bits(out_weight, ("dp", "seq"), 0)
     attn_grad = lax.dot_general(
         grad_rows, whole_weight, (((1,), (1,)), ((), ())), preferred_element_type=jnp.float32
     )

time: 235 us -> 318 us (1.35)
  waiting for transfers between devices: 73.5 us -> 140 us
  other arithmetic: 21.5 us -> 37.5 us
  between operations: 18.4 us -> 5.12 us
  starting transfers between devices: 28.3 us -> 35.8 us
  local copies, waits for them, and re-layouts: 32.5 us -> 37.4 us
    ppermute x0 -> x5, waiting for transfers between devices: none -> 110 us  [gather_by_bits(): theirs = lax.ppermute(grown, axis, [(d, d ^ reach) for d in range(ways)])]
    all_gather x1 -> x0, waiting for transfers between devices: 39.2 us -> none  [shards(): whole_weight = lax.all_gather(out_weight, ('dp', 'seq'), axis=0, tiled=True)]
    select_n x0 -> x4, other arithmetic: none -> 9.69 us  [gather_by_bits(): grown = jnp.where(here & reach == 0, mine_first, theirs_first)]
    ppermute x0 -> x5, starting transfers between devices: none -> 9.01 us  [gather_by_bits(): theirs = lax.ppermute(grown, axis, [(d, d ^ reach) for d in range(ways)])]
    dot_general x4, matrix products: 10.9 us -> 2.12 us  [shards(): jnp.einsum('gts,tgd->sd', probs_low, grad_group, preferred_element_type=j...]
    unnamed x98 -> x76, local copies, waits for them, and re-layouts: 16.7 us -> 22.3 us
    dot_general x4, matrix products: 4.2 us -> 9.43 us  [shards(): jnp.einsum('tgd,sd->gts', grad_group, value_group, preferred_element_type...]
    unnamed x2 -> x4, other arithmetic: 2.21 us -> 7.11 us
  transfers between devices with their start and end apart: 13 -> 17, of which waited for: 6 -> 8; matrix products, arithmetic and copies ran while one was open for 21% -> 19% of each run, Pallas kernels for 0% -> 0%
where the time goes in v1:
time: 318 us; the launch traced here: 316 us
  waiting for transfers between devices  140 us (44%)
  matrix products  60.7 us (19%)
  other arithmetic  37.5 us (12%)
  local copies, waits for them, and re-layouts  37.4 us (12%)
  starting transfers between devices  35.8 us (11%)
  between operations  5.12 us (2%)
    ppermute x5, waiting for transfers between devices, gather_by_bits(): theirs = lax.ppermute(grown, axis, [(d, d ^ reach) for d in range(ways)])  110 us
    ppermute x12, waiting for transfers between devices, shifted(): return lax.ppermute(block, axis, route)  29.8 us
    ppermute x12, starting transfers between devices, shifted(): return lax.ppermute(block, axis, route)  26.8 us
    unnamed x76, local copies, waits for them, and re-layouts  22.3 us
    sub x4, matrix products, shards(): exp_scores = jnp.exp(scores - row_max)  11 us
    dot_general x4, matrix products, shards(): jnp.einsum('gts,sd->tgd', probs_low, value_group, preferred_element_type=...  9.9 us
    select_n x4, other arithmetic, gather_by_bits(): grown = jnp.where(here & reach == 0, mine_first, theirs_first)  9.69 us
    dot_general x4, matrix products, shards(): jnp.einsum('tgd,sd->gts', grad_group, value_group, preferred_element_type...  9.43 us
  transfers between devices with their start and end apart: 17, of which 8 were waited for; matrix products, arithmetic and copies ran while one was open for 19% of the time, Pallas kernels for 0%

profile of v1, /device:TPU:0, one launch (start us, length us, event | category | flops | bytes accessed | tf_op | source)
XLA Modules:
  0.0 316.2 jit_solution(12492255793993567572)
XLA Ops:
  0.6 3.0 collective-permute-start.6
  3.7 6.5 %collective-permute-done.6 = bf16[64,2048]{1,0:T(8,128)(2,1)S(1)} collective-permute-done((bf16[64,2048]{1,0:T(8,128)(2,1)}, bf16[64,2048]{1,0:T(8,128)(2,1)S(1)}, u32[]{:S(2)}, u32[]{:S(2)}) %collective-permute-start.6) | collective-permute-done | bytes 262176 | tf_op jit(solution)/shard_map/ppermute | solution.py:16
  11.3 1.9 collective-permute-start.7
  13.2 11.3 %collective-permute-done.7 = bf16[128,2048]{1,0:T(8,128)(2,1)S(1)} collective-permute-done((bf16[128,2048]{1,0:T(8,128)(2,1)S(1)}, bf16[128,2048]{1,0:T(8,128)(2,1)S(1)}, u32[]{:S(2)}, u32[]{:S(2)}) %collective-permute-start.7) | collective-permute-done | bytes 524320 | tf_op jit(solution)/shard_map/ppermute | solution.py:16
  24.8 2.6 collective-permute-start.8
  27.4 44.4 %collective-permute-done.8 = bf16[256,2048]{1,0:T(8,128)(2,1)} collective-permute-done((bf16[256,2048]{1,0:T(8,128)(2,1)S(1)}, bf16[256,2048]{1,0:T(8,128)(2,1)}, u32[]{:S(2)}, u32[]{:S(2)}) %collective-permute-start.8) | collective-permute-done | bytes 1048608 | tf_op jit(solution)/shard_map/ppermute | solution.py:16
  71.8 3.1 maximum_select_fusion.2
  75.8 2.1 collective-permute-start.5
  77.9 6.8 %collective-permute-start.4 = (bf16[256,512]{0,1:T(8,128)(2,1)}, bf16[256,512]{0,1:T(8,128)(2,1)}, u32[]{:S(2)}, u32[]{:S(2)}) collective-permute-start(bf16[256,512]{0,1:T(8,128)(2,1)} %bitcast.19), channel_id=1, source_target_pairs={{0,2},{1,3},{2,4},{3,5},{4,6},{5,7},{8,10},{9,11},{10,12},{11,13},... | collective-permute-start | bytes 786440 | tf_op jit(solution)/shard_map/ppermute | solution.py:27
  84.7 4.1 %collective-permute-start.3 = (bf16[256,512]{0,1:T(8,128)(2,1)}, bf16[256,512]{0,1:T(8,128)(2,1)}, u32[]{:S(2)}, u32[]{:S(2)}) collective-permute-start(bf16[256,512]{0,1:T(8,128)(2,1)} %bitcast.19), channel_id=1, source_target_pairs={{0,1},{1,2},{2,3},{3,4},{4,5},{5,6},{6,7},{8,9},{9,10},{10,11},{11... | collective-permute-start | bytes 786440 | tf_op jit(solution)/shard_map/ppermute | solution.py:27
  88.9 2.0 collective-permute-start.2
  90.9 5.2 %maximum_select_fusion.1 = bf16[1024,2048]{1,0:T(8,128)(2,1)} fusion(bf16[512,2048]{1,0:T(8,128)(2,1)} %collective-permute-done.9, bf16[512,2048]{1,0:T(8,128)(2,1)S(1)} %maximum_select_fusion.2, pred[]{:T(512)S(6)} %eq.16), kind=kLoop, calls=%fused_computation.5 | loop fusion | flops 18874368 | bytes 8388609 | tf_op jit(solution)/shard_map/jit(_where)/select_n | solution.py:19
  106.2 2.0 collective-permute-start.1
  109.1 2.0 collective-permute-start
  120.0 2.2 pad_maximum_fusion.4
  122.2 3.5 %fusion.92 = (f32[4,256]{1,0:T(4,128)S(1)}, f32[4,256,640]{1,2,0:T(8,128)}) fusion(pred[256,640]{0,1:T(8,128)(4,1)} %fusion.50, bf16[256,4,4,128]{0,3,2,1:T(8,128)(2,1)S(1)} %bitcast.361, bf16[640,4,128]{2,0,1:T(8,128)(2,1)S(1)} %pad_maximum_fusion.5), kind=kOutput, calls=%fused_computation.186 | convolution fusion | flops 170394240 | bytes 3215360 | tf_op jit(solution)/shard_map/sub | solution.py:85
  125.7 2.5 fusion.93
  128.1 2.6 fusion.94
  130.7 2.5 fusion.95
  133.2 2.1 fusion.48
  140.7 47.7 %collective-permute-done.10 = bf16[1024,2048]{1,0:T(8,128)(2,1)} collective-permute-done((bf16[1024,2048]{1,0:T(8,128)(2,1)}, bf16[1024,2048]{1,0:T(8,128)(2,1)}, u32[]{:S(2)}, u32[]{:S(2)}) %collective-permute-start.10) | collective-permute-done | bytes 4194336 | tf_op jit(solution)/shard_map/ppermute | solution.py:16
  188.5 7.4 %convolution_convert_fusion = bf16[2048,256]{1,0:T(8,128)(2,1)S(1)} fusion(bf16[1024,2048]{1,0:T(8,128)(2,1)} %collective-permute-done.10, bf16[1024,2048]{1,0:T(8,128)(2,1)} %maximum_select_fusion.1, pred[]{:T(512)S(6)} %eq.15, bf16[1,256,2048]{2,1,0:T(8,128)(2,1)S(1)} %copy-done), kind=kOutput, calls=%fused_computation.26 | convolution fusion | flops 2185756672 | bytes 10485761 | tf_op jit(solution)/shard_map/dot_general | solution.py:62
  197.9 1.9 copy.194
  201.5 2.0 copy.160
  203.6 2.2 multiply_reduce_fusion
  205.8 2.4 fusion.5
  208.1 2.0 fusion.41
  211.4 1.8 copy.193
  215.0 2.0 copy.151
  217.0 2.6 multiply_reduce_fusion.1
  219.6 2.4 fusion.7
  221.9 2.0 fusion.42
  225.2 1.8 copy.192
  228.8 2.0 copy.142
  230.8 2.6 multiply_reduce_fusion.2
  233.4 2.4 fusion.9
  235.7 2.0 fusion.43
  239.0 1.8 copy.191
  242.6 2.0 copy.133
  244.6 2.6 multiply_reduce_fusion.3
  247.2 2.4 fusion.11
  249.6 2.1 fusion.44
  256.8 1.8 copy.105
  263.0 8.3 %fusion.12 = bf16[1,256,2048]{2,1,0:T(8,128)(2,1)} fusion(bf16[256,2048]{0,1:T(8,128)(2,1)S(1)} %bitcast.381, bf16[1024,2048]{1,0:T(8,128)(2,1)} %collective-permute-done.10, bf16[1024,2048]{1,0:T(8,128)(2,1)} %maximum_select_fusion.1, pred[]{:T(512)S(6)} %eq.15), kind=kOutput, calls=%fused_computation.28 | convolution fusion | flops 2185756672 | bytes 10485761 | tf_op jit(solution)/shard_map/dot_general | solution.py:116
  282.9 6.0 %collective-permute-done.12 = f32[128,512]{1,0:T(8,128)} collective-permute-done((f32[128,512]{1,0:T(8,128)S(1)}, f32[128,512]{1,0:T(8,128)}, u32[]{:S(2)}, u32[]{:S(2)}) %collective-permute-start.12) | collective-permute-done | bytes 262176 | tf_op jit(solution)/shard_map/ppermute | solution.py:27
  289.9 3.7 %collective-permute-done.15 = f32[128,512]{1,0:T(8,128)} collective-permute-done((f32[128,512]{1,0:T(8,128)S(1)}, f32[128,512]{1,0:T(8,128)}, u32[]{:S(2)}, u32[]{:S(2)}) %collective-permute-start.15) | collective-permute-done | bytes 262176 | tf_op jit(solution)/shard_map/ppermute | solution.py:27
  294.6 12.5 %collective-permute-done.13 = f32[128,512]{1,0:T(8,128)S(1)} collective-permute-done((f32[128,512]{1,0:T(8,128)S(1)}, f32[128,512]{1,0:T(8,128)S(1)}, u32[]{:S(2)}, u32[]{:S(2)}) %collective-permute-start.13) | collective-permute-done | bytes 262176 | tf_op jit(solution)/shard_map/ppermute | solution.py:27
  307.8 7.6 %collective-permute-done.16 = f32[128,512]{1,0:T(8,128)S(1)} collective-permute-done((f32[128,512]{1,0:T(8,128)S(1)}, f32[128,512]{1,0:T(8,128)S(1)}, u32[]{:S(2)}, u32[]{:S(2)}) %collective-permute-start.16) | collective-permute-done | bytes 262176 | tf_op jit(solution)/shard_map/ppermute | solution.py:27
  (146 shorter events, 60.9 us)
Async XLA Ops:
  0.6 187.9 %copy-start = (bf16[1,256,2048]{2,1,0:T(8,128)(2,1)S(1)}, bf16[1,256,2048]{2,1,0:T(8,128)(2,1)}, u32[]{:S(2)}) copy-start(bf16[1,256,2048]{2,1,0:T(8,128)(2,1)} %param.11) | copy-start | bytes 3145732
  0.6 9.5 %collective-permute-start.6 = (bf16[64,2048]{1,0:T(8,128)(2,1)}, bf16[64,2048]{1,0:T(8,128)(2,1)S(1)}, u32[]{:S(2)}, u32[]{:S(2)}) collective-permute-start(bf16[64,2048]{1,0:T(8,128)(2,1)} %param.10), channel_id=1, source_target_pairs={{0,1},{1,0},{2,3},{3,2},{4,5},{5,4},{6,7},{7,6},{8,9},{9,8},{10,11... | collective-permute-start | bytes 786440 | tf_op jit(solution)/shard_map/ppermute | solution.py:16
  11.3 13.2 %collective-permute-start.7 = (bf16[128,2048]{1,0:T(8,128)(2,1)S(1)}, bf16[128,2048]{1,0:T(8,128)(2,1)S(1)}, u32[]{:S(2)}, u32[]{:S(2)}) collective-permute-start(bf16[128,2048]{1,0:T(8,128)(2,1)S(1)} %maximum_select_fusion.6), channel_id=1, source_target_pairs={{0,2},{1,3},{2,0},{3,1},{4,6},{5,7},{6,4},{7,5},{8,10},{9,11},{10,... | collective-permute-start | bytes 1572872 | tf_op jit(solution)/shard_map/ppermute | solution.py:16
  24.8 2.6 copy-start.5
  24.8 50.2 %copy-start.27 = (bf16[1,256,512]{2,1,0:T(8,128)(2,1)S(1)}, bf16[1,256,512]{2,1,0:T(8,128)(2,1)}, u32[]{:S(2)}) copy-start(bf16[1,256,512]{2,1,0:T(8,128)(2,1)} %param.7) | copy-start | bytes 786436
  24.8 47.0 %collective-permute-start.8 = (bf16[256,2048]{1,0:T(8,128)(2,1)S(1)}, bf16[256,2048]{1,0:T(8,128)(2,1)}, u32[]{:S(2)}, u32[]{:S(2)}) collective-permute-start(bf16[256,2048]{1,0:T(8,128)(2,1)S(1)} %maximum_select_fusion.5), channel_id=1, source_target_pairs={{0,4},{1,5},{2,6},{3,7},{4,0},{5,1},{6,2},{7,3},{8,12},{9,13},{10,... | collective-permute-start | bytes 3145736 | tf_op jit(solution)/shard_map/ppermute | solution.py:16
  74.9 16.0 %collective-permute-start.9 = (bf16[512,2048]{1,0:T(8,128)(2,1)S(1)}, bf16[512,2048]{1,0:T(8,128)(2,1)}, u32[]{:S(2)}, u32[]{:S(2)}) collective-permute-start(bf16[512,2048]{1,0:T(8,128)(2,1)S(1)} %maximum_select_fusion.2), channel_id=1, source_target_pairs={{0,8},{1,9},{2,10},{3,11},{4,12},{5,13},{6,14},{7,15},{8,0},{9,1},... | collective-permute-start | bytes 6291464 | tf_op jit(solution)/shard_map/ppermute | solution.py:16
  75.8 30.3 %collective-permute-start.5 = (bf16[256,512]{0,1:T(8,128)(2,1)}, bf16[256,512]{0,1:T(8,128)(2,1)}, u32[]{:S(2)}, u32[]{:S(2)}) collective-permute-start(bf16[256,512]{0,1:T(8,128)(2,1)} %bitcast.19), channel_id=1, source_target_pairs={{0,4},{1,5},{2,6},{3,7},{8,12},{9,13},{10,14},{11,15},{16,20},{17,... | collective-permute-start | bytes 786440 | tf_op jit(solution)/shard_map/ppermute | solution.py:27
  77.9 31.2 %collective-permute-start.4 = (bf16[256,512]{0,1:T(8,128)(2,1)}, bf16[256,512]{0,1:T(8,128)(2,1)}, u32[]{:S(2)}, u32[]{:S(2)}) collective-permute-start(bf16[256,512]{0,1:T(8,128)(2,1)} %bitcast.19), channel_id=1, source_target_pairs={{0,2},{1,3},{2,4},{3,5},{4,6},{5,7},{8,10},{9,11},{10,12},{11,13},... | collective-permute-start | bytes 786440 | tf_op jit(solution)/shard_map/ppermute | solution.py:27
  84.7 27.3 %collective-permute-start.3 = (bf16[256,512]{0,1:T(8,128)(2,1)}, bf16[256,512]{0,1:T(8,128)(2,1)}, u32[]{:S(2)}, u32[]{:S(2)}) collective-permute-start(bf16[256,512]{0,1:T(8,128)(2,1)} %bitcast.19), channel_id=1, source_target_pairs={{0,1},{1,2},{2,3},{3,4},{4,5},{5,6},{6,7},{8,9},{9,10},{10,11},{11... | collective-permute-start | bytes 786440 | tf_op jit(solution)/shard_map/ppermute | solution.py:27
  88.9 25.2 %collective-permute-start.2 = (bf16[256,512]{1,0:T(8,128)(2,1)}, bf16[256,512]{1,0:T(8,128)(2,1)}, u32[]{:S(2)}, u32[]{:S(2)}) collective-permute-start(bf16[256,512]{1,0:T(8,128)(2,1)} %bitcast.398), channel_id=1, source_target_pairs={{0,4},{1,5},{2,6},{3,7},{8,12},{9,13},{10,14},{11,15},{16,20},{17,... | collective-permute-start | bytes 786440 | tf_op jit(solution)/shard_map/ppermute | solution.py:27
  90.8 8.0 %copy-start.31 = (s32[1,3,8]{2,0,1:T(1,128)S(1)}, s32[1,3,8]{2,0,1:T(1,128)}, u32[]{:S(2)}) copy-start(s32[1,3,8]{2,0,1:T(1,128)} %param.9) | copy-start | bytes 292
  90.8 10.6 %copy-start.28 = (bf16[1,256,512]{2,1,0:T(8,128)(2,1)S(1)}, bf16[1,256,512]{2,1,0:T(8,128)(2,1)}, u32[]{:S(2)}) copy-start(bf16[1,256,512]{2,1,0:T(8,128)(2,1)} %param.8) | copy-start | bytes 786436
  96.0 10.1 %copy-start.29 = (bf16[1,256,512]{2,1,0:T(8,128)(2,1)S(1)}, bf16[1,256,512]{2,1,0:T(8,128)(2,1)}, u32[]{:S(2)}) copy-start(bf16[1,256,512]{2,1,0:T(8,128)(2,1)} %param.8) | copy-start | bytes 786436
  96.0 92.4 %collective-permute-start.10 = (bf16[1024,2048]{1,0:T(8,128)(2,1)}, bf16[1024,2048]{1,0:T(8,128)(2,1)}, u32[]{:S(2)}, u32[]{:S(2)}) collective-permute-start(bf16[1024,2048]{1,0:T(8,128)(2,1)} %maximum_select_fusion.1), channel_id=1, source_target_pairs={{0,16},{1,17},{2,18},{3,19},{4,20},{5,21},{6,22},{7,23},{8,24},{9,... | collective-permute-start | bytes 12582920 | tf_op jit(solution)/shard_map/ppermute | solution.py:16
  106.2 9.5 %collective-permute-start.1 = (bf16[256,512]{1,0:T(8,128)(2,1)S(1)}, bf16[256,512]{1,0:T(8,128)(2,1)}, u32[]{:S(2)}, u32[]{:S(2)}) collective-permute-start(bf16[256,512]{1,0:T(8,128)(2,1)S(1)} %bitcast.399), channel_id=1, source_target_pairs={{0,2},{1,3},{2,4},{3,5},{4,6},{5,7},{8,10},{9,11},{10,12},{11,13},... | collective-permute-start | bytes 786440 | tf_op jit(solution)/shard_map/ppermute | solution.py:27
  109.1 8.3 %collective-permute-start = (bf16[256,512]{1,0:T(8,128)(2,1)S(1)}, bf16[256,512]{1,0:T(8,128)(2,1)}, u32[]{:S(2)}, u32[]{:S(2)}) collective-permute-start(bf16[256,512]{1,0:T(8,128)(2,1)S(1)} %bitcast.400), channel_id=1, source_target_pairs={{0,1},{1,2},{2,3},{3,4},{4,5},{5,6},{6,7},{8,9},{9,10},{10,11},{11... | collective-permute-start | bytes 786440 | tf_op jit(solution)/shard_map/ppermute | solution.py:27
  120.0 10.7 %copy-start.14 = (bf16[640,4,128]{2,0,1:T(8,128)(2,1)}, bf16[640,4,128]{2,0,1:T(8,128)(2,1)S(1)}, u32[]{:S(2)}) copy-start(bf16[640,4,128]{2,0,1:T(8,128)(2,1)S(1)} %pad_maximum_fusion.5) | copy-start | bytes 1966084
  122.2 3.5 %copy-start.30 = (pred[256,640]{0,1:T(8,128)(4,1)S(1)}, pred[256,640]{0,1:T(8,128)(4,1)}, u32[]{:S(2)}) copy-start(pred[256,640]{0,1:T(8,128)(4,1)} %fusion.50) | copy-start | bytes 491524
  133.2 2.5 copy-start.13
  135.3 2.1 copy-start.12
  137.1 2.3 copy-start.11
  197.9 7.9 %copy-start.7 = (bf16[2048,256]{1,0:T(8,128)(2,1)S(1)}, bf16[2048,256]{1,0:T(8,128)(2,1)}, u32[]{:S(2)}) copy-start(bf16[2048,256]{1,0:T(8,128)(2,1)} %copy-done.6) | copy-start | bytes 3145732
  249.6 2.7 copy-start.8
  249.6 2.7 copy-start.9
  249.6 2.7 copy-start.10
  253.5 1.6 copy-start.2
  253.5 2.1 copy-start.3
  254.4 1.8 copy-start.4
  256.2 6.7 %copy-start.15 = (bf16[128,4,256]{2,0,1:T(8,128)(2,1)S(1)}, bf16[128,4,256]{2,0,1:T(8,128)(2,1)}, u32[]{:S(2)}) copy-start(bf16[128,4,256]{2,0,1:T(8,128)(2,1)} %get-tuple-element.37) | copy-start | bytes 786436
  256.2 6.7 %copy-start.16 = (bf16[128,4,256]{2,0,1:T(8,128)(2,1)S(1)}, bf16[128,4,256]{2,0,1:T(8,128)(2,1)}, u32[]{:S(2)}) copy-start(bf16[128,4,256]{2,0,1:T(8,128)(2,1)} %get-tuple-element.39) | copy-start | bytes 786436
  256.2 6.7 %copy-start.17 = (bf16[128,4,256]{2,0,1:T(8,128)(2,1)S(1)}, bf16[128,4,256]{2,0,1:T(8,128)(2,1)}, u32[]{:S(2)}) copy-start(bf16[128,4,256]{2,0,1:T(8,128)(2,1)} %get-tuple-element.41) | copy-start | bytes 786436
  256.2 6.7 %copy-start.18 = (bf16[128,4,256]{2,0,1:T(8,128)(2,1)S(1)}, bf16[128,4,256]{2,0,1:T(8,128)(2,1)}, u32[]{:S(2)}) copy-start(bf16[128,4,256]{2,0,1:T(8,128)(2,1)} %get-tuple-element.43) | copy-start | bytes 786436
  258.5 20.9 %collective-permute-start.11 = (f32[128,512]{1,0:T(8,128)}, f32[128,512]{1,0:T(8,128)}, u32[]{:S(2)}, u32[]{:S(2)}) collective-permute-start(f32[128,512]{1,0:T(8,128)} %copy.105), channel_id=1, source_target_pairs={{1,0},{2,1},{3,2},{4,3},{5,4},{6,5},{7,6},{9,8},{10,9},{11,10},{12... | collective-permute-start | bytes 786440 | tf_op jit(solution)/shard_map/ppermute | solution.py:27
  261.6 20.3 %collective-permute-start.14 = (f32[128,512]{1,0:T(8,128)}, f32[128,512]{1,0:T(8,128)}, u32[]{:S(2)}, u32[]{:S(2)}) collective-permute-start(f32[128,512]{1,0:T(8,128)} %copy.118), channel_id=1, source_target_pairs={{1,0},{2,1},{3,2},{4,3},{5,4},{6,5},{7,6},{9,8},{10,9},{11,10},{12... | collective-permute-start | bytes 786440 | tf_op jit(solution)/shard_map/ppermute | solution.py:27
  271.3 1.4 copy-start.25
  271.3 1.6 copy-start.26
  272.9 1.6 slice-start
  273.1 1.7 copy-start.20
  273.1 3.1 copy-start.19
  274.5 3.1 slice-start.1
  274.5 3.3 %copy-start.22 = (f32[128,4,128]{0,2,1:T(8,128)S(1)}, f32[128,4,128]{0,2,1:T(8,128)}, u32[]{:S(2)}) copy-start(f32[128,4,128]{0,2,1:T(8,128)} %get-tuple-element.13) | copy-start | bytes 786436
  274.5 4.8 %copy-start.21 = (f32[128,4,128]{0,2,1:T(8,128)S(1)}, f32[128,4,128]{0,2,1:T(8,128)}, u32[]{:S(2)}) copy-start(f32[128,4,128]{0,2,1:T(8,128)} %get-tuple-element.12) | copy-start | bytes 786436
  274.9 14.0 %collective-permute-start.12 = (f32[128,512]{1,0:T(8,128)S(1)}, f32[128,512]{1,0:T(8,128)}, u32[]{:S(2)}, u32[]{:S(2)}) collective-permute-start(f32[128,512]{1,0:T(8,128)S(1)} %copy.107), channel_id=1, source_target_pairs={{2,0},{3,1},{4,2},{5,3},{6,4},{7,5},{10,8},{11,9},{12,10},{13,11},... | collective-permute-start | bytes 786440 | tf_op jit(solution)/shard_map/ppermute | solution.py:27
  276.3 30.7 %collective-permute-start.13 = (f32[128,512]{1,0:T(8,128)S(1)}, f32[128,512]{1,0:T(8,128)S(1)}, u32[]{:S(2)}, u32[]{:S(2)}) collective-permute-start(f32[128,512]{1,0:T(8,128)S(1)} %copy.108), channel_id=1, source_target_pairs={{4,0},{5,1},{6,2},{7,3},{12,8},{13,9},{14,10},{15,11},{20,16},{21,... | collective-permute-start | bytes 786440 | tf_op jit(solution)/shard_map/ppermute | solution.py:27
  278.0 15.6 %collective-permute-start.15 = (f32[128,512]{1,0:T(8,128)S(1)}, f32[128,512]{1,0:T(8,128)}, u32[]{:S(2)}, u32[]{:S(2)}) collective-permute-start(f32[128,512]{1,0:T(8,128)S(1)} %copy.120), channel_id=1, source_target_pairs={{2,0},{3,1},{4,2},{5,3},{6,4},{7,5},{10,8},{11,9},{12,10},{13,11},... | collective-permute-start | bytes 786440 | tf_op jit(solution)/shard_map/ppermute | solution.py:27
  279.4 36.0 %collective-permute-start.16 = (f32[128,512]{1,0:T(8,128)S(1)}, f32[128,512]{1,0:T(8,128)S(1)}, u32[]{:S(2)}, u32[]{:S(2)}) collective-permute-start(f32[128,512]{1,0:T(8,128)S(1)} %copy.121), channel_id=1, source_target_pairs={{4,0},{5,1},{6,2},{7,3},{12,8},{13,9},{14,10},{15,11},{20,16},{21,... | collective-permute-start | bytes 786440 | tf_op jit(solution)/shard_map/ppermute | solution.py:27
  280.7 35.5 %copy-start.1 = (bf16[1,256,2048]{2,1,0:T(8,128)(2,1)S(1)}, bf16[1,256,2048]{2,1,0:T(8,128)(2,1)}, u32[]{:S(2)}) copy-start(bf16[1,256,2048]{2,1,0:T(8,128)(2,1)} %param.11) | copy-start | bytes 3145732
  (3 other events, 3.4 us)
